TPU v7x, 32 devices: a whole 2x2x4 slice. The times are simulated.
32 devices in a mesh: groups: 2 (over y), blk: 16 (over z, x, core).
Axes of the slice: x: 2, y: 2, z: 4, core: 2. Of those that a mesh axis runs over, the one named last changes fastest.
Arguments:
- test_points: bfloat16 [48, 98304], P(None, ('groups', 'blk')), parts along dimension 1, may hold values from -6 to 6
- train_points: bfloat16 [48, 16384], P(None, ('groups', 'blk')), parts along dimension 1, may hold values from -6 to 6
- update_columns: bfloat16 [64, 16384], P(None, ('groups', 'blk')), parts along dimension 1, may hold values from -0.25 to 0.25
- pattern: int32 [192, 16], P('groups'), parts along dimension 0, may hold values from -1 to 15, as said below
- lengthscales: float32 [96], P('groups'), parts along dimension 0, may hold values from 4 to 16
- frequencies: bfloat16 [48, 256], P(None, 'blk'), may hold values from -12 to 12
- phases: bfloat16 [1, 256], P(None, 'blk'), may hold values from 0 to 6.28125
- prior_weights: bfloat16 [64, 256], P(None, 'blk'), may hold values from -6 to 6
Outputs:
- samples: float32 [64, 98304], P(None, ('groups', 'blk')), parts along dimension 1
There are 2 independent parts, one for each index of `groups`. A program takes and returns all parts, laid end to end along the dimension named above; an argument that names none is the same for every part. Nothing has to cross between parts.
Inputs may be any that keep to these rules, and one draw needn't show every extreme that they name: `pattern`: row t lists distinct training blocks of 0 to 15 in its first slots and -1 in the rest; every row has one tile or more, and some row fills all 16 slots.
All inputs are finite; a program needn't handle non-finite values.
Results may differ from a plain program's by a relative error of at most 0.004.
Values may be sent and summed in bfloat16 or wider, within the bound.
A program may use at most 128 MiB of HBM per device.

v0:
```python
import functools
import math

import jax
import jax.numpy as jnp
from jax import lax
from jax.experimental import pallas as pl
from jax.experimental.pallas import tpu as pltpu
from jax.sharding import PartitionSpec as P

TB = 512
PADDED = 128
MESH = pl.DeviceIdType.MESH
LOG2E = math.log2(math.e)
COS_TERMS = [(-1.0) ** k * (2.0 * math.pi) ** (2 * k) / math.factorial(2 * k) for k in range(11)]


def three_parts(value):
    high = value.astype(jnp.bfloat16).astype(jnp.float32)
    rest = value - high
    middle = rest.astype(jnp.bfloat16).astype(jnp.float32)
    return high, middle, (rest - middle).astype(jnp.bfloat16).astype(jnp.float32)


def rows_of(first, second):
    width = first[0].shape[1] if hasattr(first[0], "shape") else second[0].shape[1]
    row = lax.broadcasted_iota(jnp.int32, (32, width), 0)
    out = jnp.zeros((32, width), jnp.float32)
    for place, part in enumerate(list(first) + list(second)):
        out = jnp.where(row == place, part, out)
    return out


def turn_cos(turns):
    f = turns - jnp.round(turns)
    z = f * f
    total = jnp.full_like(z, COS_TERMS[-1])
    for term in COS_TERMS[-2::-1]:
        total = total * z + term
    return total


def gather_kernel(
    n, test_ref, train_ref, columns_ref, scale_ref, pack_ref,
    train_aug, all_columns, test_aug, prior_ref,
    packs, blocks, small_send, small_recv, big_send, big_recv,
):
    group = lax.axis_index("groups")
    me = lax.axis_index("blk")
    feats, samples = train_ref.shape[0], columns_ref.shape[0]
    depth = pack_ref.shape[0]
    lines = n // 4
    a, b, c = me // 4, (me // 2) % 2, me % 2

    def index(a_, b_, c_):
        return (a_ * 2 + b_) * 2 + c_

    line = [index((a + k) % lines, b, c) for k in range(lines)]
    across = index(a, 1 - b, c)
    core = index(a, b, 1 - c)
    partners = line[1:] + [across, core]

    barrier = pltpu.get_barrier_semaphore()
    for other in partners:
        pl.semaphore_signal(barrier, inc=1, device_id=(group, other), device_id_type=MESH)

    scale = scale_ref[...]
    train = (train_ref[...].astype(jnp.float32) / scale).astype(jnp.bfloat16)
    blocks[pl.ds(me, 1), :feats, :] = train[None]
    blocks[pl.ds(me, 1), feats:, :] = columns_ref[...][None]
    packs[pl.ds(me, 1)] = pack_ref[...][None]
    pl.semaphore_wait(barrier, len(partners))

    def copy(buffer, send, recv, source, target, number):
        return pltpu.make_async_remote_copy(
            src_ref=buffer.at[pl.ds(source, 1)], dst_ref=buffer.at[pl.ds(source, 1)],
            send_sem=send.at[number], recv_sem=recv.at[source],
            device_id=(group, target), device_id_type=MESH,
        )

    sent = []

    def start(small, source, target):
        number = counts[small]
        counts[small] += 1
        one = (copy(packs, small_send, small_recv, source, target, number) if small
               else copy(blocks, big_send, big_recv, source, target, number))
        one.start()
        sent.append(one)

    def arrive(small, source):
        if small:
            copy(packs, small_send, small_recv, source, me, 0).wait_recv()
        else:
            copy(blocks, big_send, big_recv, source, me, 0).wait_recv()

    counts = {True: 0, False: 0}

    def first_wave(small):
        for other in line[1:]:
            start(small, me, other)
        start(small, me, across)
        start(small, me, core)

    def line_arrivals(small):
        for k in range(1, lines):
            source = line[lines - k]
            arrive(small, source)
            start(small, source, across)
            start(small, source, core)

    def across_arrivals(small):
        for k in range(lines):
            source = index((a - k) % lines, 1 - b, c)
            arrive(small, source)
            start(small, source, core)

    def core_arrivals(small):
        for k in range(lines):
            arrive(small, index((a - k) % lines, b, 1 - c))
            arrive(small, index((a - k) % lines, 1 - b, 1 - c))

    first_wave(True)
    first_wave(False)

    chunks = test_ref.shape[1] // TB

    def make_test(i, _):
        at = pl.ds(pl.multiple_of(i * TB, TB), TB)
        scaled = (test_ref[:, at].astype(jnp.float32) / scale).astype(jnp.bfloat16)
        wide = scaled.astype(jnp.float32)
        norm = 5.0 * jnp.sum(wide * wide, axis=0, keepdims=True)
        tail = rows_of([1.0, 1.0, 1.0], three_parts(norm))
        test_aug[:feats, at] = scaled
        test_aug[feats:2 * feats, at] = scaled
        test_aug[2 * feats:, at] = tail.astype(jnp.bfloat16)
        return 0

    lax.fori_loop(0, chunks, make_test, 0)

    line_arrivals(True)
    across_arrivals(True)
    core_arrivals(True)
    line_arrivals(False)

    total = n * depth
    factor = math.sqrt(2.0 / total)
    step = min(total, 256)
    held = step // depth

    def make_prior(i, _):
        at = pl.ds(pl.multiple_of(i * TB, TB), TB)

        def part(first):
            pack = packs[pl.ds(first, held)].reshape(step, 2 * PADDED)
            turns = jnp.dot(
                pack[:, :PADDED], test_aug[:, at], preferred_element_type=jnp.float32
            ) * (0.5 / math.pi)
            features = turn_cos(turns).astype(jnp.bfloat16)
            return lax.dot_general(
                pack[:, PADDED:], features, (((0,), (0,)), ((), ())),
                preferred_element_type=jnp.float32,
            )[:samples]

        if total == step:
            result = part(0)
        else:
            result = lax.fori_loop(
                0, total // step, lambda p, run: run + part(p * held),
                jnp.zeros((samples, TB), jnp.float32),
            )
        prior_ref[:, at] = result * factor
        return 0

    lax.fori_loop(0, chunks, make_prior, 0)

    across_arrivals(False)
    core_arrivals(False)

    def make_train(s, _):
        block = blocks[pl.ds(s, 1)][0]
        wide = block[:feats].astype(jnp.float32)
        norm = 5.0 * jnp.sum(wide * wide, axis=0, keepdims=True)
        double = -10.0 * wide
        high = double.astype(jnp.bfloat16).astype(jnp.float32)
        tail = rows_of(three_parts(norm), [1.0, 1.0, 1.0])
        whole = jnp.concatenate([high, double - high, tail], axis=0)
        train_aug[pl.ds(s, 1)] = whole.T.astype(jnp.bfloat16)[None]
        all_columns[pl.ds(s, 1)] = block[feats:][None]
        return 0

    lax.fori_loop(0, n, make_train, 0)
    for one in sent:
        one.wait_send()


def matern_thrice(dist):
    dist = jnp.maximum(dist, 1e-30)
    q = dist * lax.rsqrt(dist)
    bell = jnp.exp2(q * (-LOG2E)).astype(jnp.bfloat16)
    q = q.astype(jnp.bfloat16)
    three = jnp.bfloat16(3.0)
    return ((q + three) * q + three) * bell


UNROLL = 4


def tile_kernel(
    pattern_ref, train_aug, all_columns, test_aug, prior_ref, out_ref,
    sums, even, odd, row_list, block_list,
):
    me = lax.axis_index("blk")
    rows = test_aug.shape[1] // TB
    slots = pattern_ref.shape[1]

    def list_row(row, count):
        def more(state):
            slot, _ = state
            return jnp.logical_and(
                slot < slots, pattern_ref[me * rows + row, jnp.minimum(slot, slots - 1)] >= 0
            )

        def put(state):
            slot, place = state
            row_list[place] = row
            block_list[place] = pattern_ref[me * rows + row, slot]
            return slot + 1, place + 1

        return lax.while_loop(more, put, (0, count))[1]

    count = lax.fori_loop(0, rows, list_row, 0)
    for extra in range(UNROLL + 1):
        row_list[count + extra] = rows
        block_list[count + extra] = 0
    sums[...] = jnp.zeros_like(sums)

    def front(place, held):
        row = jnp.minimum(row_list[place], rows - 1)
        at = pl.ds(pl.multiple_of(row * TB, TB), TB)
        held[...] = matern_thrice(jnp.dot(
            train_aug[block_list[place]], test_aug[:, at], preferred_element_type=jnp.float32
        ))

    def back(place, held):
        sums[row_list[place]] += jnp.dot(
            all_columns[block_list[place]], held[...], preferred_element_type=jnp.float32
        )

    held = (even, odd)
    front(0, even)

    def step(i, _):
        first = i * UNROLL
        for u in range(UNROLL):
            front(first + u + 1, held[(u + 1) % 2])
            back(first + u, held[u % 2])
        return 0

    lax.fori_loop(0, (count + UNROLL - 1) // UNROLL, step, 0)
    for row in range(rows):
        at = pl.ds(row * TB, TB)
        out_ref[:, at] = prior_ref[:, at] + sums[row] * (1.0 / 3.0)


def as_column(row):
    size = row.shape[1]
    across = lax.broadcasted_iota(jnp.int32, (size, size), 1)
    down = lax.broadcasted_iota(jnp.int32, (size, size), 0)
    return jnp.sum(jnp.where(across == down, row, 0.0), axis=1, keepdims=True)


def dense_kernel(
    n, test_ref, train_ref, columns_ref, scale_ref, freq_ref, phase_ref, weight_ref, pattern_ref,
    out_ref,
    packs, blocks, test_aug, train_aug, sums, masks, even, odd,
    small_send, small_recv, big_send, big_recv,
):
    group = lax.axis_index("groups")
    me = lax.axis_index("blk")
    feats, samples = train_ref.shape[0], columns_ref.shape[0]
    depth = freq_ref.shape[0]
    rows = test_ref.shape[1] // TB
    lines = n // 4
    a, b, c = me // 4, (me // 2) % 2, me % 2

    def index(a_, b_, c_):
        return (a_ * 2 + b_) * 2 + c_

    line = [index((a + k) % lines, b, c) for k in range(lines)]
    across = index(a, 1 - b, c)
    core = index(a, b, 1 - c)
    partners = line[1:] + [across, core]

    barrier = pltpu.get_barrier_semaphore()
    for other in partners:
        pl.semaphore_signal(barrier, inc=1, device_id=(group, other), device_id_type=MESH)

    scale = as_column(scale_ref[...])
    train = (train_ref[...].astype(jnp.float32) / scale).astype(jnp.bfloat16)
    blocks[pl.ds(me, 1), :feats, :] = train[None]
    blocks[pl.ds(me, 1), feats:, :] = columns_ref[...][None]
    lane = lax.broadcasted_iota(jnp.int32, (depth, PADDED), 1)
    phase = as_column(phase_ref[...].astype(jnp.float32))
    pack = jnp.where(lane == 2 * feats, phase, 0.0).astype(jnp.bfloat16)
    packs[pl.ds(me, 1), :, :PADDED] = pack[None]
    packs[pl.ds(me, 1), :, :feats] = freq_ref[...][None]
    packs[pl.ds(me, 1), :, PADDED:] = jnp.zeros((1, depth, PADDED), jnp.bfloat16)
    packs[pl.ds(me, 1), :, PADDED:PADDED + samples] = weight_ref[...][None]
    pl.semaphore_wait(barrier, len(partners))

    def copy(buffer, send, recv, source, target, number):
        return pltpu.make_async_remote_copy(
            src_ref=buffer.at[pl.ds(source, 1)], dst_ref=buffer.at[pl.ds(source, 1)],
            send_sem=send.at[number], recv_sem=recv.at[source],
            device_id=(group, target), device_id_type=MESH,
        )

    def small(source, target, number):
        return copy(packs, small_send, small_recv, source, target, number)

    def big(source, target, number):
        return copy(blocks, big_send, big_recv, source, target, number)

    for number, other in enumerate(partners):
        small(me, other, number).start()
    for number, other in enumerate(partners):
        big(me, other, number).start()
    copies = 4 * lines - 1

    def make_test(i, _):
        at = pl.ds(pl.multiple_of(i * TB, TB), TB)
        scaled = (test_ref[:, at].astype(jnp.float32) / scale).astype(jnp.bfloat16)
        wide = scaled.astype(jnp.float32)
        norm = 5.0 * jnp.sum(wide * wide, axis=0, keepdims=True)
        tail = rows_of([1.0, 1.0, 1.0], three_parts(norm))
        test_aug[:feats, at] = scaled
        test_aug[feats:2 * feats, at] = scaled
        test_aug[2 * feats:, at] = tail.astype(jnp.bfloat16)
        return 0

    lax.fori_loop(0, rows, make_test, 0)

    slots, all_rows = pattern_ref.shape
    wide_pattern = pattern_ref[...].astype(jnp.float32)
    place = lax.broadcasted_iota(jnp.int32, (slots, all_rows), 1)
    number = lax.broadcasted_iota(jnp.int32, (slots, n), 1).astype(jnp.float32)
    for row in range(rows):
        named = jnp.sum(
            jnp.where(place == me * rows + row, wide_pattern, 0.0), axis=1, keepdims=True
        )
        found = jnp.sum(jnp.where(named == number, 1.0 / 3.0, 0.0), axis=0, keepdims=True)
        masks[row] = jnp.broadcast_to(as_column(found), (n, TB))

    sums[...] = jnp.zeros_like(sums)
    odd[...] = jnp.zeros_like(odd)
    held = (even, odd)

    def origin(k):
        kind, far = k // lines, k % lines
        swap_b, swap_c = kind % 2, kind // 2
        return index(
            (a + lines - far) % lines, b + swap_b - 2 * b * swap_b, c + swap_c - 2 * c * swap_c
        )

    def front(row):
        at = pl.ds(row * TB, TB)
        held[row % 2][...] = matern_thrice(
            jnp.dot(train_aug[...], test_aug[:, at], preferred_element_type=jnp.float32)
        )

    def back(source, row):
        product = jnp.dot(
            blocks[pl.ds(source, 1), feats:, :][0], held[row % 2][...],
            preferred_element_type=jnp.float32,
        )
        sums[row] += product * masks[row, pl.ds(source, 1), :]

    def one_block(k, _):
        source = origin(k)
        before = origin(jnp.maximum(k - 1, 0))

        @pl.when(k > 0)
        def _():
            big(source, me, 0).wait_recv()

        @pl.when(jnp.logical_and(k > 0, k < lines))
        def _():
            big(source, across, lines + 2 * k - 1).start()
            big(source, core, lines + 2 * k).start()
            small(source, me, 0).wait_recv()
            small(source, across, lines + 2 * k - 1).start()
            small(source, core, lines + 2 * k).start()

        @pl.when(jnp.logical_and(k >= lines, k < 2 * lines))
        def _():
            big(source, core, 2 * lines - 1 + k).start()
            small(source, me, 0).wait_recv()
            small(source, core, 2 * lines - 1 + k).start()

        @pl.when(k >= 2 * lines)
        def _():
            small(source, me, 0).wait_recv()

        wide = blocks[pl.ds(source, 1), :feats, :][0].astype(jnp.float32)
        norm = 5.0 * jnp.sum(wide * wide, axis=0, keepdims=True)
        double = -10.0 * wide
        high = double.astype(jnp.bfloat16).astype(jnp.float32)
        tail = rows_of(three_parts(norm), [1.0, 1.0, 1.0])
        whole = jnp.concatenate([high, double - high, tail], axis=0)
        train_aug[...] = whole.T.astype(jnp.bfloat16)
        for row in range(rows):
            front(row)
            if row == 0:
                back(before, rows - 1)
            else:
                back(source, row - 1)
        return 0

    lax.fori_loop(0, n, one_block, 0)
    back(origin(n - 1), rows - 1)

    factor = math.sqrt(2.0 / (n * depth))
    every = packs[...].reshape(n * depth, 2 * PADDED)

    def finish(i, _):
        at = pl.ds(pl.multiple_of(i * TB, TB), TB)
        turns = jnp.dot(
            every[:, :PADDED], test_aug[:, at], preferred_element_type=jnp.float32
        ) * (0.5 / math.pi)
        prior = lax.dot_general(
            every[:, PADDED:], turn_cos(turns).astype(jnp.bfloat16), (((0,), (0,)), ((), ())),
            preferred_element_type=jnp.float32,
        )[:samples]
        out_ref[:, at] = prior * factor + sums[pl.ds(i, 1)][0]
        return 0

    lax.fori_loop(0, rows, finish, 0)
    for number in range(copies):
        small(me, core, number).wait_send()
        big(me, core, number).wait_send()


def dense_on_device(
    test_points, train_points, update_columns, pattern, lengthscales, frequencies, phases,
    prior_weights,
):
    n = lax.axis_size("blk")
    feats, points = test_points.shape
    samples = update_columns.shape[0]
    depth = frequencies.shape[1]
    rows = points // TB
    vmem = pl.BlockSpec(memory_space=pltpu.VMEM)
    copies = n - 1
    return pl.pallas_call(
        functools.partial(dense_kernel, n),
        out_shape=jax.ShapeDtypeStruct((samples, points), jnp.float32),
        in_specs=[vmem] * 8,
        out_specs=vmem,
        scratch_shapes=[
            pltpu.VMEM((n, depth, 2 * PADDED), jnp.bfloat16),
            pltpu.VMEM((n, feats + samples, TB), jnp.bfloat16),
            pltpu.VMEM((PADDED, points), jnp.bfloat16),
            pltpu.VMEM((TB, PADDED), jnp.bfloat16),
            pltpu.VMEM((rows, samples, TB), jnp.float32),
            pltpu.VMEM((rows, n, TB), jnp.float32),
            pltpu.VMEM((TB, TB), jnp.bfloat16),
            pltpu.VMEM((TB, TB), jnp.bfloat16),
            pltpu.SemaphoreType.DMA((copies,)),
            pltpu.SemaphoreType.DMA((n,)),
            pltpu.SemaphoreType.DMA((copies,)),
            pltpu.SemaphoreType.DMA((n,)),
        ],
        compiler_params=pltpu.CompilerParams(
            collective_id=1, has_side_effects=True, vmem_limit_bytes=56 * 2**20
        ),
        name="samples",
    )(
        test_points, train_points, update_columns, lengthscales[None, :], frequencies.T, phases,
        prior_weights.T, pattern.T,
    )


def on_device(
    test_points, train_points, update_columns, pattern, lengthscales, frequencies, phases,
    prior_weights,
):
    n = lax.axis_size("blk")
    feats, points = test_points.shape
    samples = update_columns.shape[0]
    depth = frequencies.shape[1]
    pack = jnp.concatenate(
        [
            frequencies.T, jnp.zeros((depth, feats), jnp.bfloat16), phases.T,
            jnp.zeros((depth, PADDED - 2 * feats - 1), jnp.bfloat16), prior_weights.T,
            jnp.zeros((depth, PADDED - samples), jnp.bfloat16),
        ],
        axis=1,
    )
    vmem = pl.BlockSpec(memory_space=pltpu.VMEM)
    copies = n // 4 + 1 + 2 * (n // 4 - 1) + n // 4
    train_aug, all_columns, test_aug, prior = pl.pallas_call(
        functools.partial(gather_kernel, n),
        out_shape=(
            jax.ShapeDtypeStruct((n, TB, PADDED), jnp.bfloat16),
            jax.ShapeDtypeStruct((n, samples, TB), jnp.bfloat16),
            jax.ShapeDtypeStruct((PADDED, points), jnp.bfloat16),
            jax.ShapeDtypeStruct((samples, points), jnp.float32),
        ),
        in_specs=[vmem] * 5,
        out_specs=(vmem,) * 4,
        scratch_shapes=[
            pltpu.VMEM((n, depth, 2 * PADDED), jnp.bfloat16),
            pltpu.VMEM((n, feats + samples, TB), jnp.bfloat16),
            pltpu.SemaphoreType.DMA((copies,)),
            pltpu.SemaphoreType.DMA((n,)),
            pltpu.SemaphoreType.DMA((copies,)),
            pltpu.SemaphoreType.DMA((n,)),
        ],
        compiler_params=pltpu.CompilerParams(
            collective_id=0, has_side_effects=True, vmem_limit_bytes=56 * 2**20
        ),
        name="gather_and_prior",
    )(test_points, train_points, update_columns, lengthscales[:, None], pack)
    return pl.pallas_call(
        tile_kernel,
        out_shape=jax.ShapeDtypeStruct((samples, points), jnp.float32),
        in_specs=[pl.BlockSpec(memory_space=pltpu.SMEM)] + [vmem] * 4,
        out_specs=vmem,
        scratch_shapes=[
            pltpu.VMEM((points // TB + 1, samples, TB), jnp.float32),
            pltpu.VMEM((TB, TB), jnp.bfloat16),
            pltpu.VMEM((TB, TB), jnp.bfloat16),
            pltpu.SMEM((points // TB * pattern.shape[1] + 2 * UNROLL,), jnp.int32),
            pltpu.SMEM((points // TB * pattern.shape[1] + 2 * UNROLL,), jnp.int32),
        ],
        compiler_params=pltpu.CompilerParams(vmem_limit_bytes=56 * 2**20),
        name="tiles",
    )(pattern, train_aug, all_columns, test_aug, prior)


def either(test_points, train_points, update_columns, pattern, *others):
    rows = test_points.shape[1] // TB
    dense = pattern.shape[1] >= lax.axis_size("blk") and rows % 2 == 0
    run = dense_on_device if dense else on_device
    return run(test_points, train_points, update_columns, pattern, *others)


def solution(mesh):
    placed = (
        P(None, ("groups", "blk")),
        P(None, ("groups", "blk")),
        P(None, ("groups", "blk")),
        P("groups", None),
        P("groups"),
        P(None, "blk"),
        P(None, "blk"),
        P(None, "blk"),
    )
    return jax.shard_map(
        either, mesh=mesh, in_specs=placed, out_specs=P(None, ("groups", "blk")), check_vma=False
    )
```

profile of v0, /device:TPU:0, one launch (start us, length us, event | category | flops | bytes accessed | tf_op | source)
XLA Modules:
  0.0 61.2 jit_solution(8952801697132658921)
XLA Ops:
  0.0 59.2 %samples.1 = f32[64,3072]{1,0:T(8,128)} custom-call(bf16[48,3072]{1,0:T(8,128)(2,1)} %test_ref.1, bf16[48,512]{1,0:T(8,128)(2,1)} %train_ref.1, bf16[64,512]{1,0:T(8,128)(2,1)} %columns_ref.1, f32[1,48]{1,0:T(1,128)} %bitcast.7, bf16[16,48]{1,0:T(8,128)(2,1)} %bitcast.5, bf16[1,16]{1,0:T(2,128)(2,1)} %phase_ref.1, bf16[16,64]{1,0:T(8,128)(2,1)} %bitcast.6, ...), custom_call_target="tpu_custom_call" | custom-call | tf_op jit(solution)/shard_map/samples/pallas_call | solution.py:455
  59.2 2.1 %copy.10 = f32[64,3072]{1,0:T(8,128)} copy(f32[64,3072]{1,0:T(8,128)} %samples.1) | data formatting | bytes 1572864
where the time goes:
time: 61.5 us; the launch traced here: 61.2 us
  Pallas kernels  59.2 us (96%)
  local copies, waits for them, and re-layouts  2.07 us (3%)
    pallas_call x1, Pallas kernels, dense_on_device(): pl.pallas_call(functools.partial(dense_kernel, n), out_shape=jax.ShapeDty...  59.2 us
    unnamed x1, local copies, waits for them, and re-layouts  2.07 us

commit v1 on v0

--- a/solution.py
+++ b/solution.py
@@ -12,6 +12,7 @@
 PADDED = 128
 MESH = pl.DeviceIdType.MESH
 LOG2E = math.log2(math.e)
+NORM = 5.0 / 3.0
 COS_TERMS = [(-1.0) ** k * (2.0 * math.pi) ** (2 * k) / math.factorial(2 * k) for k in range(11)]
 
 
@@ -129,7 +130,7 @@
         at = pl.ds(pl.multiple_of(i * TB, TB), TB)
         scaled = (test_ref[:, at].astype(jnp.float32) / scale).astype(jnp.bfloat16)
         wide = scaled.astype(jnp.float32)
-        norm = 5.0 * jnp.sum(wide * wide, axis=0, keepdims=True)
+        norm = NORM * jnp.sum(wide * wide, axis=0, keepdims=True)
         tail = rows_of([1.0, 1.0, 1.0], three_parts(norm))
         test_aug[:feats, at] = scaled
         test_aug[feats:2 * feats, at] = scaled
@@ -180,8 +181,8 @@
     def make_train(s, _):
         block = blocks[pl.ds(s, 1)][0]
         wide = block[:feats].astype(jnp.float32)
-        norm = 5.0 * jnp.sum(wide * wide, axis=0, keepdims=True)
-        double = -10.0 * wide
+        norm = NORM * jnp.sum(wide * wide, axis=0, keepdims=True)
+        double = (-2.0 * NORM) * wide
         high = double.astype(jnp.bfloat16).astype(jnp.float32)
         tail = rows_of(three_parts(norm), [1.0, 1.0, 1.0])
         whole = jnp.concatenate([high, double - high, tail], axis=0)
@@ -194,13 +195,11 @@
         one.wait_send()
 
 
-def matern_thrice(dist):
+def matern(dist):
     dist = jnp.maximum(dist, 1e-30)
-    q = dist * lax.rsqrt(dist)
-    bell = jnp.exp2(q * (-LOG2E)).astype(jnp.bfloat16)
-    q = q.astype(jnp.bfloat16)
-    three = jnp.bfloat16(3.0)
-    return ((q + three) * q + three) * bell
+    w = dist * lax.rsqrt(dist)
+    bell = jnp.exp2(w * (-LOG2E * math.sqrt(3.0)))
+    return (((w + math.sqrt(3.0)) * w + 1.0) * bell).astype(jnp.bfloat16)
 
 
 UNROLL = 4
@@ -238,7 +237,7 @@
     def front(place, held):
         row = jnp.minimum(row_list[place], rows - 1)
         at = pl.ds(pl.multiple_of(row * TB, TB), TB)
-        held[...] = matern_thrice(jnp.dot(
+        held[...] = matern(jnp.dot(
             train_aug[block_list[place]], test_aug[:, at], preferred_element_type=jnp.float32
         ))
 
@@ -260,7 +259,7 @@
     lax.fori_loop(0, (count + UNROLL - 1) // UNROLL, step, 0)
     for row in range(rows):
         at = pl.ds(row * TB, TB)
-        out_ref[:, at] = prior_ref[:, at] + sums[row] * (1.0 / 3.0)
+        out_ref[:, at] = prior_ref[:, at] + sums[row]
 
 
 def as_column(row):
@@ -290,7 +289,7 @@
     line = [index((a + k) % lines, b, c) for k in range(lines)]
     across = index(a, 1 - b, c)
     core = index(a, b, 1 - c)
-    partners = line[1:] + [across, core]
+    partners = [core, across] + line[1:]
 
     barrier = pltpu.get_barrier_semaphore()
     for other in partners:
@@ -332,7 +331,7 @@
         at = pl.ds(pl.multiple_of(i * TB, TB), TB)
         scaled = (test_ref[:, at].astype(jnp.float32) / scale).astype(jnp.bfloat16)
         wide = scaled.astype(jnp.float32)
-        norm = 5.0 * jnp.sum(wide * wide, axis=0, keepdims=True)
+        norm = NORM * jnp.sum(wide * wide, axis=0, keepdims=True)
         tail = rows_of([1.0, 1.0, 1.0], three_parts(norm))
         test_aug[:feats, at] = scaled
         test_aug[feats:2 * feats, at] = scaled
@@ -349,15 +348,21 @@
         named = jnp.sum(
             jnp.where(place == me * rows + row, wide_pattern, 0.0), axis=1, keepdims=True
         )
-        found = jnp.sum(jnp.where(named == number, 1.0 / 3.0, 0.0), axis=0, keepdims=True)
+        found = jnp.sum(jnp.where(named == number, 1.0, 0.0), axis=0, keepdims=True)
         masks[row] = jnp.broadcast_to(as_column(found), (n, TB))
 
     sums[...] = jnp.zeros_like(sums)
     odd[...] = jnp.zeros_like(odd)
     held = (even, odd)
 
+    def kind_and_far(k):
+        rest = k - 3
+        kind = jnp.where(k < 3, (2 * k) % 3, jnp.minimum(rest // (lines - 1), 3))
+        far = jnp.where(k < 3, 0, rest - kind * (lines - 1) + jnp.where(kind < 3, 1, 0))
+        return kind, far
+
     def origin(k):
-        kind, far = k // lines, k % lines
+        kind, far = kind_and_far(k)
         swap_b, swap_c = kind % 2, kind // 2
         return index(
             (a + lines - far) % lines, b + swap_b - 2 * b * swap_b, c + swap_c - 2 * c * swap_c
@@ -365,7 +370,7 @@
 
     def front(row):
         at = pl.ds(row * TB, TB)
-        held[row % 2][...] = matern_thrice(
+        held[row % 2][...] = matern(
             jnp.dot(train_aug[...], test_aug[:, at], preferred_element_type=jnp.float32)
         )
 
@@ -384,27 +389,29 @@
         def _():
             big(source, me, 0).wait_recv()
 
-        @pl.when(jnp.logical_and(k > 0, k < lines))
+        kind, far = kind_and_far(k)
+
+        @pl.when(jnp.logical_and(kind == 0, k > 0))
         def _():
-            big(source, across, lines + 2 * k - 1).start()
-            big(source, core, lines + 2 * k).start()
+            big(source, across, lines + 2 * far - 1).start()
+            big(source, core, lines + 2 * far).start()
             small(source, me, 0).wait_recv()
-            small(source, across, lines + 2 * k - 1).start()
-            small(source, core, lines + 2 * k).start()
-
-        @pl.when(jnp.logical_and(k >= lines, k < 2 * lines))
+            small(source, across, lines + 2 * far - 1).start()
+            small(source, core, lines + 2 * far).start()
+
+        @pl.when(kind == 1)
         def _():
-            big(source, core, 2 * lines - 1 + k).start()
+            big(source, core, 3 * lines - 1 + far).start()
             small(source, me, 0).wait_recv()
-            small(source, core, 2 * lines - 1 + k).start()
-
-        @pl.when(k >= 2 * lines)
+            small(source, core, 3 * lines - 1 + far).start()
+
+        @pl.when(kind >= 2)
         def _():
             small(source, me, 0).wait_recv()
 
         wide = blocks[pl.ds(source, 1), :feats, :][0].astype(jnp.float32)
-        norm = 5.0 * jnp.sum(wide * wide, axis=0, keepdims=True)
-        double = -10.0 * wide
+        norm = NORM * jnp.sum(wide * wide, axis=0, keepdims=True)
+        double = (-2.0 * NORM) * wide
         high = double.astype(jnp.bfloat16).astype(jnp.float32)
         tail = rows_of(three_parts(norm), [1.0, 1.0, 1.0])
         whole = jnp.concatenate([high, double - high, tail], axis=0)

time: 61.5 us -> 61.1 us (level)
  no operation moved by 1% of the time
where the time goes in v1:
time: 61.1 us; the launch traced here: 61 us
  Pallas kernels  58.9 us (96%)
  local copies, waits for them, and re-layouts  2.07 us (3%)
    pallas_call x1, Pallas kernels, dense_on_device(): pl.pallas_call(functools.partial(dense_kernel, n), out_shape=jax.ShapeDty...  58.9 us
    unnamed x1, local copies, waits for them, and re-layouts  2.07 us

profile of v1, /device:TPU:0, one launch (start us, length us, event | category | flops | bytes accessed | tf_op | source)
XLA Modules:
  0.0 61.0 jit_solution(2492841324988868699)
XLA Ops:
  0.0 58.9 %samples.1 = f32[64,3072]{1,0:T(8,128)} custom-call(bf16[48,3072]{1,0:T(8,128)(2,1)} %test_ref.1, bf16[48,512]{1,0:T(8,128)(2,1)} %train_ref.1, bf16[64,512]{1,0:T(8,128)(2,1)} %columns_ref.1, f32[1,48]{1,0:T(1,128)} %bitcast.7, bf16[16,48]{1,0:T(8,128)(2,1)} %bitcast.5, bf16[1,16]{1,0:T(2,128)(2,1)} %phase_ref.1, bf16[16,64]{1,0:T(8,128)(2,1)} %bitcast.6, ...), custom_call_target="tpu_custom_call" | custom-call | tf_op jit(solution)/shard_map/samples/pallas_call | solution.py:462
  58.9 2.1 %copy.10 = f32[64,3072]{1,0:T(8,128)} copy(f32[64,3072]{1,0:T(8,128)} %samples.1) | data formatting | bytes 1572864

commit v2 on v1

--- a/solution.py
+++ b/solution.py
@@ -13,7 +13,9 @@
 MESH = pl.DeviceIdType.MESH
 LOG2E = math.log2(math.e)
 NORM = 5.0 / 3.0
-COS_TERMS = [(-1.0) ** k * (2.0 * math.pi) ** (2 * k) / math.factorial(2 * k) for k in range(11)]
+SIN_TERMS = [
+    (-1.0) ** k * (2.0 * math.pi) ** (2 * k + 1) / math.factorial(2 * k + 1) for k in range(7)
+]
 
 
 def three_parts(value):
@@ -33,12 +35,12 @@
 
 
 def turn_cos(turns):
-    f = turns - jnp.round(turns)
-    z = f * f
-    total = jnp.full_like(z, COS_TERMS[-1])
-    for term in COS_TERMS[-2::-1]:
+    g = 0.25 - jnp.abs(turns - jnp.round(turns))
+    z = g * g
+    total = z * SIN_TERMS[-1] + SIN_TERMS[-2]
+    for term in SIN_TERMS[-3::-1]:
         total = total * z + term
-    return total
+    return total * g
 
 
 def gather_kernel(
@@ -199,7 +201,7 @@
     dist = jnp.maximum(dist, 1e-30)
     w = dist * lax.rsqrt(dist)
     bell = jnp.exp2(w * (-LOG2E * math.sqrt(3.0)))
-    return (((w + math.sqrt(3.0)) * w + 1.0) * bell).astype(jnp.bfloat16)
+    return ((dist + (w * math.sqrt(3.0) + 1.0)) * bell).astype(jnp.bfloat16)
 
 
 UNROLL = 4

time: 61.1 us -> 57.7 us (0.944)
  Pallas kernels: 58.9 us -> 55.5 us
    pallas_call x1, Pallas kernels: 58.9 us -> 55.5 us  [dense_on_device(): pl.pallas_call(functools.partial(dense_kernel, n), out_shape=jax.ShapeDty...]
where the time goes in v2:
time: 57.7 us; the launch traced here: 57.6 us
  Pallas kernels  55.5 us (96%)
  local copies, waits for them, and re-layouts  2.07 us (4%)
    pallas_call x1, Pallas kernels, dense_on_device(): pl.pallas_call(functools.partial(dense_kernel, n), out_shape=jax.ShapeDty...  55.5 us
    unnamed x1, local copies, waits for them, and re-layouts  2.07 us

profile of v2, /device:TPU:0, one launch (start us, length us, event | category | flops | bytes accessed | tf_op | source)
XLA Modules:
  0.0 57.6 jit_solution(6536937553943167198)
XLA Ops:
  0.0 55.5 %samples.1 = f32[64,3072]{1,0:T(8,128)} custom-call(bf16[48,3072]{1,0:T(8,128)(2,1)} %test_ref.1, bf16[48,512]{1,0:T(8,128)(2,1)} %train_ref.1, bf16[64,512]{1,0:T(8,128)(2,1)} %columns_ref.1, f32[1,48]{1,0:T(1,128)} %bitcast.7, bf16[16,48]{1,0:T(8,128)(2,1)} %bitcast.5, bf16[1,16]{1,0:T(2,128)(2,1)} %phase_ref.1, bf16[16,64]{1,0:T(8,128)(2,1)} %bitcast.6, ...), custom_call_target="tpu_custom_call" | custom-call | tf_op jit(solution)/shard_map/samples/pallas_call | solution.py:464
  55.5 2.1 %copy.10 = f32[64,3072]{1,0:T(8,128)} copy(f32[64,3072]{1,0:T(8,128)} %samples.1) | data formatting | bytes 1572864
